TPU v7x, 256 devices: a whole 4x4x8 slice. The times are simulated.
256 devices in a mesh: pp: 8 (over x, core), ep: 32 (over z, y).
Axes of the slice: x: 4, y: 4, z: 8, core: 2. Of those that a mesh axis runs over, the one named last changes fastest.
Arguments:
- tokens: bfloat16 [4096, 7168], P('ep'), may hold values from -6 to 6
- expert_ids: int32 [4096, 4], P('ep'), may hold values from 0 to 31, all different within a row; in each aligned block of 128 rows (0 to 127, 128 to 255, ...) at most 24 rows name the same one
- route_score: float32 [4096, 4], P('ep'), may hold values from 0.05 to 1
- gate_weight: bfloat16 [32, 7168, 2048], P('ep', None, 'pp'), may hold values from -0.0625 to 0.0625
- up_weight: bfloat16 [32, 7168, 2048], P('ep', None, 'pp'), may hold values from -0.0625 to 0.0625
- down_weight: bfloat16 [32, 2048, 7168], P('ep', 'pp'), may hold values from -0.125 to 0.125
Outputs:
- layer_output: bfloat16 [4096, 7168], P('ep', 'pp')
Inputs may be any that keep to these rules, and one draw needn't show every extreme that they name: `expert_ids`: each row names 4 different experts. Among the 128 tokens of one index of ep, no expert is named by more than 24 of them, a bound that some block reaches.
All inputs are finite; a program needn't handle non-finite values.
Results may differ from a plain program's by a relative error of at most 0.019.
Values may be sent and summed in bfloat16 or wider, within the bound.
A program may use at most 192 MiB of HBM per device.

v0:
```python
import jax
import jax.numpy as jnp
from jax import lax
from jax.sharding import PartitionSpec as P


def slot_target(block_ids, expert_count, capacity):
    flattened = block_ids.reshape(-1)
    one_hot = (flattened[:, None] == jnp.arange(expert_count, dtype=jnp.int32)[None, :]).astype(
        jnp.int32
    )
    earlier = jnp.cumsum(one_hot, axis=0, dtype=jnp.int32) - one_hot
    position = jnp.sum(earlier * one_hot, axis=1, dtype=jnp.int32)
    return flattened * capacity + position


def slot_owner(target, pair_count, buffer_size):
    owners = jnp.full((buffer_size,), pair_count, jnp.int32)
    return owners.at[target].set(jnp.arange(pair_count, dtype=jnp.int32))


def per_device(tokens, expert_ids, route_score, gate_weight, up_weight, down_weight):
    expert_count = lax.axis_size("ep")
    tok_count, model_width = tokens.shape
    chosen = expert_ids.shape[1]
    capacity = 3 * tok_count * chosen // (2 * expert_count)
    pair_count = tok_count * chosen
    route_weight = route_score / jnp.sum(route_score, axis=1, keepdims=True)
    target = slot_target(expert_ids, expert_count, capacity)
    owners = slot_owner(target, pair_count, expert_count * capacity)
    filled = owners < pair_count
    source = jnp.where(filled, owners // chosen, 0)
    gate_local = gate_weight[0]
    up_local = up_weight[0]
    down_local = down_weight[0]
    outgoing = jnp.where(filled[:, None], tokens[source], jnp.zeros((), jnp.bfloat16))
    arrived = lax.all_to_all(
        outgoing.reshape(expert_count, capacity, model_width),
        "ep",
        split_axis=0,
        concat_axis=0,
        tiled=True,
    )
    arrived_rows = arrived.reshape(-1, model_width)
    gate_sum = jnp.dot(arrived_rows, gate_local, preferred_element_type=jnp.float32)
    up_sum = jnp.dot(arrived_rows, up_local, preferred_element_type=jnp.float32)
    hidden = (jax.nn.silu(gate_sum) * up_sum).astype(jnp.bfloat16)
    expert_part = jnp.dot(hidden, down_local, preferred_element_type=jnp.float32).astype(
        jnp.bfloat16
    )
    returned = lax.all_to_all(
        expert_part.reshape(expert_count, capacity, model_width),
        "ep",
        split_axis=0,
        concat_axis=0,
        tiled=True,
    )
    picked = (
        returned.reshape(-1, model_width)[target]
        .astype(jnp.float32)
        .reshape(tok_count, chosen, model_width)
    )
    blended = jnp.sum(picked * route_weight[:, :, None], axis=1)
    result = lax.psum_scatter(blended.astype(jnp.bfloat16), "pp", scatter_dimension=1, tiled=True)
    return result


def solution(mesh):
    placed = (
        P("ep", None),
        P("ep", None),
        P("ep", None),
        P("ep", None, "pp"),
        P("ep", None, "pp"),
        P("ep", "pp", None),
    )
    return jax.shard_map(
        per_device, mesh=mesh, in_specs=placed, out_specs=P("ep", "pp"), check_vma=False
    )
```

profile of v0, /device:TPU:1, one launch (start us, length us, event | category | flops | bytes accessed | tf_op | source)
XLA Modules:
  0.0 660.4 jit_solution(2059080036760212507)
XLA Ops:
  6.5 0.0 copy-start
  6.5 0.9 copy.14
  7.5 0.1 eq.29
  7.6 0.1 eq.25
  7.7 0.7 broadcast_multiply_fusion
  8.4 1.2 reduce-window.6
  9.5 0.2 slice_reduce_fusion
  9.8 0.1 copy.13
  9.9 0.1 mul.36
  10.0 0.1 fusion.21
  10.2 2.4 scatter_custom_fusion
  12.7 0.1 broadcast_in_dim.25
  12.8 0.0 copy-done
  12.8 9.5 %gather_fusion = bf16[768,7168]{1,0:T(8,128)(2,1)} fusion(bf16[128,7168]{1,0:T(8,128)(2,1)S(1)} %copy-done, s32[1024]{0:T(1024)S(1)} %pad_clamp_fusion.1), kind=kCustom, calls=%fused_computation | custom fusion | bytes 22023168 | tf_op jit(solution)/shard_map/gather | solution.py:36
  22.2 5.9 broadcast_select_fusion
  28.1 0.0 copy-start.4
  28.1 252.9 %all_to_all.10 = bf16[32,24,7168]{2,1,0:T(8,128)(2,1)S(1)} all-to-all(bf16[32,24,7168]{2,1,0:T(8,128)(2,1)S(1)} %broadcast_select_fusion), channel_id=1, replica_groups=mesh['pp'=8,'ep'=32] {'ep'}, dimensions={0} | all-to-all | bytes 22020096 | tf_op jit(solution)/shard_map/all_to_all | solution.py:37
  281.0 0.0 copy-start.2
  281.0 4.2 copy-done.2
  285.2 0.0 copy-done.4
  285.2 3.0 fusion.3
  288.2 18.9 %convolution_convert_fusion = bf16[768,7168]{1,0:T(8,128)(2,1)} fusion(bf16[1,256,7168]{2,1,0:T(8,128)(2,1)} %param.11, bf16[768,7168]{1,0:T(8,128)(2,1)} %bitcast.47, bf16[1,7168,256]{2,1,0:T(8,128)(2,1)} %param.10, f32[768,256]{1,0:T(8,128)S(1)} %fusion.3), kind=kOutput, calls=%fused_computation.4 | convolution fusion | flops 5643829248 | bytes 30146560 | tf_op jit(solution)/shard_map/dot_general | solution.py:48
  307.1 0.0 copy-start.3
  307.1 5.7 all-to-all-start.1
  312.8 0.2 reduce-scatter.4.cloned.1.call-start
  313.0 0.0 copy-done.3
  313.1 0.1 copy.17
  313.2 240.6 %all-to-all-done.1 = bf16[32,24,7168]{2,1,0:T(8,128)(2,1)} async-done(((bf16[32,24,7168]{2,1,0:T(8,128)(2,1)}), bf16[32,24,7168]{2,1,0:T(8,128)(2,1)}, u32[]{:S(2)}, u32[]{:S(2)}) %all-to-all-start.1) | async-done | bytes 11010080 | tf_op jit(solution)/shard_map/all_to_all | solution.py:51
  553.7 19.4 %gather_fusion.1 = bf16[512,7168]{1,0:T(8,128)(2,1)} fusion(bf16[768,7168]{1,0:T(8,128)(2,1)} %bitcast.9, s32[1024]{0:T(1024)S(1)} %pad_clamp_fusion), kind=kCustom, calls=%fused_computation.1 | custom fusion | bytes 14682112 | tf_op jit(solution)/shard_map/gather | solution.py:59
  573.1 0.0 copy-start.1
  573.1 14.1 %reshape.73 = f32[128,4,7168]{2,1,0:T(4,128)} reshape(bf16[512,7168]{1,0:T(8,128)(2,1)} %gather_fusion.1) | data formatting | bytes 22020096 | tf_op jit(solution)/shard_map/convert_element_type | solution.py:60
  587.2 13.5 %multiply_reduce_fusion = bf16[128,7168]{1,0:T(8,128)(2,1)} fusion(f32[128,4,7168]{2,1,0:T(4,128)} %reshape.73, f32[128,4]{1,0:T(8,128)S(1)} %copy.17), kind=kLoop, calls=%fused_computation.3 | loop fusion | flops 6422528 | bytes 16517120 | tf_op jit(solution)/shard_map/reduce_sum | solution.py:63
  600.6 3.9 copy.18
  604.5 0.0 reduce-scatter.4.cloned.1.call-update
  604.6 47.3 %reduce-scatter.4.cloned.1.call-done = bf16[896,128]{1,0:T(8,128)(2,1)} async-done(((bf16[7168,128]{1,0:T(8,128)(2,1)}), bf16[896,128]{1,0:T(8,128)(2,1)}) %reduce-scatter.4.cloned.1.call-update) | async-done | bytes 229392
  651.8 1.8 copy.19
  653.6 0.0 copy-done.1
  (11 shorter events, 0.1 us)
Async XLA Ops:
  6.5 6.2 copy-start
  28.1 257.0 %copy-start.4 = (bf16[1,7168,256]{2,1,0:T(8,128)(2,1)S(1)}, bf16[1,7168,256]{2,1,0:T(8,128)(2,1)}, u32[]{:S(2)}) copy-start(bf16[1,7168,256]{2,1,0:T(8,128)(2,1)} %param.9) | copy-start | bytes 11010052
  281.0 4.2 copy-start.2
  307.1 6.0 copy-start.3
  307.1 246.7 %all-to-all-start.1 = ((bf16[32,24,7168]{2,1,0:T(8,128)(2,1)}), bf16[32,24,7168]{2,1,0:T(8,128)(2,1)}, u32[]{:S(2)}, u32[]{:S(2)}) async-start(bf16[32,24,7168]{2,1,0:T(8,128)(2,1)} %bitcast.45), calls=%async_computation.1 | async-start | bytes 22020096 | tf_op jit(solution)/shard_map/all_to_all | solution.py:51
  312.8 339.0 %reduce-scatter.4.cloned.1.call-start = ((), (), s32[]{:S(2)}) async-start(), calls=%async_computation.3 | async-start | bytes 2064384
  573.1 80.5 %copy-start.1 = (bf16[128,7168]{1,0:T(8,128)(2,1)S(1)}, bf16[128,7168]{1,0:T(8,128)(2,1)}, u32[]{:S(2)}) copy-start(bf16[128,7168]{1,0:T(8,128)(2,1)} %param.6) | copy-start | bytes 5505028
Sparse Core Ops, SparseCore 0:
  604.7 47.1 reduce-scatter.3
where the time goes:
time: 663 us; the launch traced here: 660 us
  waiting for transfers between devices  288 us (43%)
  blocking collectives  253 us (38%)
  local copies, waits for them, and re-layouts  57 us (9%)
  matrix products  21.9 us (3%)
  other arithmetic  21.4 us (3%)
  between operations  13.5 us (2%)
    all_to_all x1, blocking collectives, per_device(): lax.all_to_all(outgoing.reshape(expert_count, capacity, model_width), 'ep...  253 us
    all_to_all x1, waiting for transfers between devices, per_device(): lax.all_to_all(expert_part.reshape(expert_count, capacity, model_width),...  241 us
    unnamed x2, waiting for transfers between devices  47.3 us
    gather x1, local copies, waits for them, and re-layouts, per_device(): returned.reshape(-1, model_width)[target].astype(jnp.float32)  19.4 us
    dot_general x1, matrix products, per_device(): jnp.dot(hidden, down_local, preferred_element_type=jnp.float32)  18.9 us
    convert_element_type x1, local copies, waits for them, and re-layouts, per_device(): picked = returned.reshape(-1, model_width)[target].astype(jnp.float32).re...  14.1 us
    reduce_sum x1, other arithmetic, per_device(): blended = jnp.sum(picked * route_weight[:, :, None], axis=1)  13.5 us
  transfers between devices with their start and end apart: 2, of which 2 were waited for; matrix products, arithmetic and copies ran while one was open for 0% of the time, Pallas kernels for 0%

commit v1 on v0

v1 whole, which is shorter than its diff:
```python
import jax
import jax.numpy as jnp
from jax import lax
from jax.experimental import pallas as pl
from jax.experimental.pallas import tpu as pltpu
from jax.sharding import PartitionSpec as P

MESH = pl.DeviceIdType.MESH
F32, BF16 = jnp.float32, jnp.bfloat16
D, REGION, CW = 7168, 1792, 256
TOK, CAP, NE, TOPK = 128, 24, 32, 4
NX, NZ, NY = 4, 8, 4
ROWS = NY * 4 * CAP
YR = 4 * CAP
HALF = ROWS // 2
NA, ND = 5, 8
NCH = NA + ND
NPIECE = 7


def kernel(meta_ref, tok, gate, up, down, out_ref, mine, metas, wgu, wd, T, GS, XA, acc, H, S, SWT, PX, RA, FX, Q, ZR, ZF, O,
           w_loc, w_send, w_recv, m_send, m_recv, z_send, z_recv, y_send, y_recv, x_send, x_recv,
           rx_send, rx_recv, ry_send, ry_recv, rz_send, rz_recv, o_send, o_recv):
    pp, ep = lax.axis_index("pp"), lax.axis_index("ep")
    x, c, z, y = lax.div(pp, 2), lax.rem(pp, 2), lax.div(ep, NY), lax.rem(ep, NY)
    sgn = 2 * c - 1

    def dev(dx=0, dz=0, dy=0):
        return (lax.rem(x + dx + NX, NX) * 2 + c, lax.rem(z + dz + NZ, NZ) * NY + lax.rem(y + dy, NY))

    def remote(src, dst, ss, rs, device):
        return pltpu.make_async_remote_copy(src_ref=src, dst_ref=dst, send_sem=ss, recv_sem=rs, device_id=device,
                                            device_id_type=MESH)

    sib = (x * 2 + 1 - c, ep)
    bar = pltpu.get_barrier_semaphore()
    for k in range(1, 8):
        pl.semaphore_signal(bar, inc=1, device_id=(lax.rem(pp + k, 8), ep), device_id_type=MESH)
        pl.semaphore_signal(bar, inc=1, device_id=dev(dz=k), device_id_type=MESH)
    for k in range(1, 4):
        pl.semaphore_signal(bar, inc=1, device_id=dev(dy=k), device_id_type=MESH)

    local = [
        pltpu.make_async_copy(gate, wgu.at[c], w_loc.at[0]),
        pltpu.make_async_copy(up, wgu.at[2 + c], w_loc.at[1]),
        pltpu.make_async_copy(down, wd.at[pl.ds(pl.multiple_of(c * 256, 256), 256)], w_loc.at[2]),
    ]
    for cp in local:
        cp.start()

    ids, score = meta_ref[0:4, :], meta_ref[4:8, :]
    e_iota = lax.broadcasted_iota(jnp.int32, (NE, TOK), 0).astype(F32)
    hot = [(e_iota == ids[k:k + 1, :]).astype(F32) for k in range(TOPK)]
    count = hot[0] + hot[1] + hot[2] + hot[3]
    before = (lax.broadcasted_iota(jnp.int32, (TOK, TOK), 0) < lax.broadcasted_iota(jnp.int32, (TOK, TOK), 1)).astype(F32)
    earlier = jnp.dot(count.astype(BF16), before.astype(BF16), preferred_element_type=F32)
    pos = [jnp.sum(h * earlier, axis=0, keepdims=True) for h in hot]
    mine[0:4, :] = ids * CAP + jnp.concatenate(pos, axis=0)
    mine[4:8, :] = score / jnp.sum(score, axis=0, keepdims=True)

    pl.semaphore_wait(bar, 17)

    def meta_copy(s):
        return remote(mine, metas.at[s], m_send.at[s], m_recv.at[s], dev(dz=sgn * (s + c)))

    @pl.when(c == 0)
    def _():
        metas[0] = mine[...]

    @pl.when(c == 1)
    def _():
        meta_copy(0).start()

    for s in range(1, 4):
        meta_copy(s).start()

    def col_a(r, j):
        return pl.multiple_of(REGION * r + CW * (j + lax.div(j, 3)), CW)

    def col_d(d):
        return pl.multiple_of(REGION * lax.div(d, 2) + CW * (3 + 3 * lax.rem(d, 2)), CW)

    def col(j):
        return pl.multiple_of(jnp.where(j < NA, col_a(x, j), col_d(j - NA)), CW)

    def slot(j):
        return jnp.where(j < NA, x * NA + j, 3 * NA + j)

    def stage(s):
        return pl.ds(s * TOK, TOK)

    def first_hop(j):
        return remote(tok.at[:, pl.ds(col(j), CW)], T.at[j, stage(0)], z_send.at[0, j], z_recv.at[0, j], dev(dz=sgn))

    def hop(s, j):
        return remote(T.at[j, stage(s - 1)], T.at[j, stage(s)], z_send.at[s, j], z_recv.at[s, j], dev(dz=sgn))

    def y_rows(k):
        return pl.ds(pl.multiple_of(k * YR, 32), YR)

    def y_copy(dy, j):
        there = lax.rem(y + dy, NY)
        return remote(GS.at[j, y_rows(there)], XA.at[slot(j), y_rows(y)], y_send.at[dy - 1, j], y_recv.at[dy - 1, j], dev(dy=dy))

    def x_copy(i, j):
        if i < 2:
            return remote(XA.at[x * NA + j], XA.at[x * NA + j], x_send.at[i, j], x_recv.at[i, j], dev(dx=1 - 2 * i))
        away = lax.rem(x + (3 if i == 2 else 1), NX) * NA + j
        part = pl.ds(0, HALF) if i == 2 else pl.ds(HALF, HALF)
        return remote(XA.at[away, part], XA.at[away, part], x_send.at[i, j], x_recv.at[i, j], dev(dx=1 if i == 2 else -1))

    def gate_up(sl, w_row):
        @pl.loop(0, 4)
        def _(i):
            acc[i] += jnp.dot(XA[sl], wgu[i, pl.ds(w_row, CW), :], preferred_element_type=F32)

    def within(j, n):
        return jnp.logical_and(j >= 0, j < n)

    w_copies = [
        remote(gate, wgu.at[c], w_send.at[0], w_recv.at[0], sib),
        remote(up, wgu.at[2 + c], w_send.at[1], w_recv.at[1], sib),
        remote(down, wd.at[pl.ds(pl.multiple_of(c * 256, 256), 256)], w_send.at[2], w_recv.at[2], sib),
    ]

    XS, XF, XM, LAG = 6, 8, 10, 6
    steps = max(NCH + LAG, XM + 2 * NA - 1)

    def dispatch(t, carry):
        @pl.when(t < NCH)
        def _():
            @pl.when(c == 0)
            def _():
                pltpu.make_async_copy(tok.at[:, pl.ds(col(t), CW)], T.at[t, stage(0)], z_recv.at[0, t]).start()

            @pl.when(c == 1)
            def _():
                first_hop(t).start()

        for h in range(3):
            j = t - 1 - h

            @pl.when(within(j, NCH))
            def _():
                first_hop(j).wait_recv() if h == 0 else hop(h, j).wait_recv()
                hop(h + 1, j).start()

        @pl.when(t == 0)
        def _():
            for cp in w_copies:
                cp.start()
            acc[...] = jnp.zeros_like(acc)

        @pl.when(t == 2)
        def _():
            @pl.when(c == 1)
            def _():
                meta_copy(0).wait()

            for s in range(1, 4):
                meta_copy(s).wait()
            p_iota = lax.broadcasted_iota(jnp.int32, (CAP, TOK), 0).astype(F32)
            empty = jnp.zeros((CAP, TOK), F32)
            for s in range(4):
                picks, weighted = [], []
                for yy in range(NY):
                    key = p_iota + ((z * NY + yy) * CAP).astype(F32)
                    eq = [(metas[s, k:k + 1, :] == key).astype(F32) for k in range(TOPK)]
                    pick = eq[0] + eq[1] + eq[2] + eq[3]
                    wpick = sum(eq[k] * metas[s, 4 + k:5 + k, :] for k in range(TOPK))
                    picks += [pick if s2 == s else empty for s2 in range(4)]
                    weighted += [wpick if s2 == s else empty for s2 in range(4)]
                S[:, s * TOK:(s + 1) * TOK] = jnp.concatenate(picks, axis=0).astype(BF16)
                SWT[s * TOK:(s + 1) * TOK, :] = jnp.concatenate(weighted, axis=0).T.astype(BF16)

        j_pick = t - 4

        @pl.when(within(j_pick, NCH))
        def _():
            hop(3, j_pick).wait_recv()
            GS[j_pick] = jnp.dot(S[...], T[j_pick], preferred_element_type=F32).astype(BF16)
            for dy in range(1, 4):
                y_copy(dy, j_pick).start()
            XA[slot(j_pick), y_rows(y), :] = GS[j_pick, y_rows(y), :]

        @pl.when(t == LAG)
        def _():
            for cp in local:
                cp.wait()
            for cp in w_copies[:2]:
                cp.wait()

        ja = t - XS

        @pl.when(jnp.logical_and(within(ja, 2 * NA), lax.rem(ja + 64, 2) == 0))
        def _():
            j = lax.div(ja, 2)
            for dy in range(1, 4):
                y_copy(dy, j).wait()
            x_copy(0, j).start()
            x_copy(1, j).start()

        jf = t - XF

        @pl.when(jnp.logical_and(within(jf, 2 * NA), lax.rem(jf + 64, 2) == 0))
        def _():
            j = lax.div(jf, 2)
            x_copy(0, j).wait()
            x_copy(2, j).start()
            x_copy(1, j).wait()
            x_copy(3, j).start()

        jd = t - LAG

        @pl.when(jnp.logical_and(jd >= NA, jd < NCH))
        def _():
            for dy in range(1, 4):
                y_copy(dy, jd).wait()
            gate_up(3 * NA + jd, col_d(jd - NA))

        jm = t - XM

        @pl.when(jnp.logical_and(within(jm, 2 * NA), lax.rem(jm + 64, 2) == 0))
        def _():
            j = lax.div(jm, 2)
            x_copy(2, j).wait()
            x_copy(3, j).wait()

            @pl.loop(0, NX)
            def _(r):
                gate_up(r * NA + j, col_a(r, j))

        for h in range(4):
            j = t - 2 - h

            @pl.when(within(j, NCH))
            def _():
                if h == 0:
                    pl.when(c == 1)(lambda: first_hop(j).wait_send())
                else:
                    hop(h, j).wait_send()

        return carry

    lax.fori_loop(0, steps, dispatch, 0)

    for i in range(2):
        g = acc[i]
        H[:, i * 256:(i + 1) * 256] = (g / (1.0 + jnp.exp(-g)) * acc[2 + i]).astype(BF16)
    w_copies[2].wait()

    right, left, anti = lax.rem(x + 1, NX), lax.rem(x + 3, NX), lax.rem(x + 2, NX)
    lo, hi = pl.ds(0, HALF), pl.ds(HALF, HALF)

    def rx_copy(i, j):
        src, dst, dx = [
            (PX.at[j, anti, lo], RA.at[0, j], 1),
            (PX.at[j, anti, hi], RA.at[1, j], -1),
            (PX.at[j, right, hi], FX.at[0, j, hi], 1),
            (PX.at[j, left, lo], FX.at[1, j, lo], -1),
            (PX.at[j, right, lo], FX.at[0, j, lo], 1),
            (PX.at[j, left, hi], FX.at[1, j, hi], -1),
        ][i]
        return remote(src, dst, rx_send.at[i, j], rx_recv.at[i, j], dev(dx=dx))

    def ry_copy(dy, j):
        there = lax.rem(y + dy, NY)
        return remote(GS.at[j, y_rows(there)], Q.at[j, y_rows(y)], ry_send.at[dy - 1, j], ry_recv.at[dy - 1, j], dev(dy=dy))

    def rz_copy(s, j):
        if s == 0:
            return remote(T.at[j, stage(0)], ZF.at[j], rz_send.at[0, j], rz_recv.at[0, j], dev(dz=-sgn))
        return remote(T.at[j, stage(s)], ZR.at[j, stage(s - 1)], rz_send.at[s, j], rz_recv.at[s, j], dev(dz=-sgn))

    def local_chunk(q):
        return jnp.where(q < ND, NA + q, q - ND)

    def out_copy(h, j):
        d = j - NA
        region = jnp.where(j < NA, x, lax.div(jnp.maximum(d, 0), 2))
        i = jnp.where(j < NA, j + lax.div(j, 3), 3 + 3 * lax.rem(jnp.maximum(d, 0), 2))
        p = 2 * i + h
        owner = lax.div(p, NPIECE)
        place = lax.rem(p, NPIECE)
        there = region * 2 + owner
        return there, place, remote(ZF.at[j, :, pl.ds(h * 128, 128)], O.at[place, pp], o_send.at[h, j], o_recv.at[place, pp],
                                    (there, ep))

    def back(t, carry):
        @pl.when(jnp.logical_and(t < 2 * NA, lax.rem(t, 2) == 0))
        def _():
            j = lax.div(t, 2)

            @pl.loop(0, NX)
            def _(r):
                PX[j, r] = jnp.dot(H[...], wd[:, pl.ds(col_a(r, j), CW)], preferred_element_type=F32).astype(BF16)

            for i in range(4):
                rx_copy(i, j).start()

        @pl.when(jnp.logical_and(within(t - 2, 2 * NA), lax.rem(t, 2) == 0))
        def _():
            j = lax.div(t - 2, 2)
            rx_copy(0, j).wait()
            PX[j, right, lo, :] = (PX[j, right, lo, :].astype(F32) + RA[0, j].astype(F32)).astype(BF16)
            rx_copy(4, j).start()
            rx_copy(1, j).wait()
            PX[j, left, hi, :] = (PX[j, left, hi, :].astype(F32) + RA[1, j].astype(F32)).astype(BF16)
            rx_copy(5, j).start()

        @pl.when(jnp.logical_and(within(t - 4, 2 * NA), lax.rem(t, 2) == 0))
        def _():
            j = lax.div(t - 4, 2)
            for i in range(2, 6):
                rx_copy(i, j).wait()
            GS[j] = (PX[j, x].astype(F32) + FX[0, j].astype(F32) + FX[1, j].astype(F32)).astype(BF16)

        @pl.when(t < NCH)
        def _():
            j = local_chunk(t)

            @pl.when(t < ND)
            def _():
                GS[j] = jnp.dot(H[...], wd[:, pl.ds(col_d(t), CW)], preferred_element_type=F32).astype(BF16)

            for dy in range(1, 4):
                ry_copy(dy, j).start()
            Q[j, y_rows(y), :] = GS[j, y_rows(y), :]

        @pl.when(within(t - 2, NCH))
        def _():
            j = local_chunk(t - 2)
            for dy in range(1, 4):
                ry_copy(dy, j).wait()
            T[j] = jnp.dot(SWT[...], Q[j], preferred_element_type=F32).astype(BF16)
            rz_copy(3, j).start()

        for s in (2, 1, 0):
            @pl.when(within(t - 5 + s, NCH))
            def _():
                j = local_chunk(t - 5 + s)
                rz_copy(s + 1, j).wait()
                total = (T[j, stage(s), :].astype(F32) + ZR[j, stage(s), :].astype(F32)).astype(BF16)
                if s > 0:
                    T[j, stage(s), :] = total
                    rz_copy(s, j).start()
                else:
                    @pl.when(c == 0)
                    def _():
                        ZF[j] = total

                    @pl.when(c == 1)
                    def _():
                        T[j, stage(0), :] = total
                        rz_copy(0, j).start()

        @pl.when(within(t - 6, NCH))
        def _():
            j = local_chunk(t - 6)

            @pl.when(c == 1)
            def _():
                rz_copy(0, j).wait()

            for h in range(2):
                there, place, cp = out_copy(h, j)

                @pl.when(there != pp)
                def _():
                    cp.start()

                @pl.when(there == pp)
                def _():
                    O[place, pp] = ZF[j, :, h * 128:(h + 1) * 128]

        return carry

    lax.fori_loop(0, NCH + 6, back, 0)

    def sent(j, carry):
        for h in range(2):
            there, place, cp = out_copy(h, j)

            @pl.when(there != pp)
            def _():
                cp.wait_send()
        return carry

    lax.fori_loop(0, NCH, sent, 0)

    for place in range(NPIECE):
        p = c * NPIECE + place
        i = lax.div(p, 2)
        summed = lax.rem(i, 3) == 0

        def arrived(src):
            remote(O.at[place, src], O.at[place, src], o_send.at[0, 0], o_recv.at[place, src], sib).wait_recv()

        is_d = jnp.logical_and(i > 0, summed)

        @pl.when(is_d)
        def _():
            for k in range(1, 8):
                arrived(lax.rem(pp + k, 8))
            total = O[place, 0].astype(F32)
            for k in range(1, 8):
                total += O[place, k].astype(F32)
            out_ref[:, place * 128:(place + 1) * 128] = total.astype(BF16)

        @pl.when(jnp.logical_not(is_d))
        def _():
            arrived(x * 2 + 1 - c)
            out_ref[:, place * 128:(place + 1) * 128] = (O[place, x * 2].astype(F32) + O[place, x * 2 + 1].astype(F32)).astype(BF16)


def per_device(tokens, expert_ids, route_score, gate_weight, up_weight, down_weight):
    meta = jnp.concatenate([expert_ids.astype(F32), route_score], axis=1).T
    vm, dma = pltpu.VMEM, pltpu.SemaphoreType.DMA
    hbm = pl.BlockSpec(memory_space=pl.ANY)
    return pl.pallas_call(
        kernel,
        out_shape=jax.ShapeDtypeStruct((TOK, NPIECE * 128), BF16),
        in_specs=[pl.BlockSpec(memory_space=vm), hbm, hbm, hbm, hbm],
        out_specs=pl.BlockSpec(memory_space=vm),
        scratch_shapes=[
            vm((8, TOK), F32), vm((4, 8, TOK), F32),
            vm((4, D, 256), BF16), vm((512, D), BF16),
            vm((NCH, 4 * TOK, CW), BF16),
            vm((NCH, ROWS, CW), BF16),
            vm((4 * NA + ND, ROWS, CW), BF16),
            vm((4, ROWS, 256), F32), vm((ROWS, 512), BF16),
            vm((ROWS, 4 * TOK), BF16), vm((4 * TOK, ROWS), BF16),
            vm((NA, NX, ROWS, CW), BF16),
            vm((2, NA, HALF, CW), BF16), vm((2, NA, ROWS, CW), BF16),
            vm((NCH, ROWS, CW), BF16),
            vm((NCH, 3 * TOK, CW), BF16), vm((NCH, TOK, CW), BF16),
            vm((NPIECE, 8, TOK, 128), BF16),
            dma((3,)), dma((3,)), dma((3,)), dma((4,)), dma((4,)),
            dma((4, NCH)), dma((4, NCH)), dma((3, NCH)), dma((3, NCH)), dma((4, NA)), dma((4, NA)),
            dma((6, NA)), dma((6, NA)), dma((3, NCH)), dma((3, NCH)), dma((4, NCH)), dma((4, NCH)),
            dma((2, NCH)), dma((NPIECE, 8)),
        ],
        compiler_params=pltpu.CompilerParams(collective_id=0, has_side_effects=True, vmem_limit_bytes=62 * 2**20),
        name="moe",
    )(meta, tokens, gate_weight[0], up_weight[0], down_weight[0])


def solution(mesh):
    placed = (
        P("ep", None),
        P("ep", None),
        P("ep", None),
        P("ep", None, "pp"),
        P("ep", None, "pp"),
        P("ep", "pp", None),
    )
    return jax.shard_map(
        per_device, mesh=mesh, in_specs=placed, out_specs=P("ep", "pp"), check_vma=False
    )
```

time: 663 us -> 150 us (0.23)
  waiting for transfers between devices: 288 us -> 0 us
  blocking collectives: 253 us -> 0 us
  Pallas kernels: 0 us -> 146 us
  local copies, waits for them, and re-layouts: 57 us -> 1.65 us
  matrix products: 21.9 us -> 0 us
  other arithmetic: 21.4 us -> 1.96 us
  between operations: 13.5 us -> 0.01 us
    all_to_all x1 -> x0, blocking collectives: 253 us -> none  [per_device(): lax.all_to_all(outgoing.reshape(expert_count, capacity, model_width), 'ep...]
    all_to_all x1 -> x0, waiting for transfers between devices: 241 us -> none  [per_device(): lax.all_to_all(expert_part.reshape(expert_count, capacity, model_width),...]
    pallas_call x0 -> x1, Pallas kernels: none -> 146 us  [per_device(): pl.pallas_call(kernel, out_shape=jax.ShapeDtypeStruct((TOK, NPIECE * 128)...]
    unnamed x2 -> x0, waiting for transfers between devices: 47.3 us -> none
    gather x2 -> x0, local copies, waits for them, and re-layouts: 28.8 us -> none  [the longest x1 19.4 us: per_device(): returned.reshape(-1, model_width)[target].astype(jnp.float32)]
    dot_general x2 -> x0, matrix products: 21.9 us -> none  [the longest x1 18.9 us: per_device(): jnp.dot(hidden, down_local, preferred_element_type=jnp.float32)]
    convert_element_type x1 -> x0, local copies, waits for them, and re-layouts: 14.1 us -> none  [per_device(): picked = returned.reshape(-1, model_width)[target].astype(jnp.float32).re...]
    reduce_sum x3 -> x0, other arithmetic: 13.6 us -> none  [the longest x1 13.5 us: per_device(): blended = jnp.sum(picked * route_weight[:, :, None], axis=1)]
  transfers between devices with their start and end apart: 2 -> 0, of which waited for: 2 -> 0; matrix products, arithmetic and copies ran while one was open for 0% -> 0% of each run, Pallas kernels for 0% -> 0%
where the time goes in v1:
time: 150 us
  Pallas kernels  146 us (97%)
  other arithmetic  1.96 us (1%)
  local copies, waits for them, and re-layouts  1.65 us (1%)
    pallas_call x1, Pallas kernels, per_device(): pl.pallas_call(kernel, out_shape=jax.ShapeDtypeStruct((TOK, NPIECE * 128)...  146 us

profile of v1, /device:TPU:1, one launch (start us, length us, event | category | flops | bytes accessed | tf_op | source)
XLA Modules:
  0.0 149.5 jit_solution(1697121516224641439)
XLA Ops:
  0.0 0.7 convert_element_type.3
  0.7 1.3 maximum_bitcast_fusion.meta_ref
  2.0 145.9 %moe.1 = bf16[128,896]{1,0:T(8,128)(2,1)} custom-call(f32[8,128]{1,0:T(8,128)} %maximum_bitcast_fusion.meta_ref, bf16[128,7168]{1,0:T(8,128)(2,1)} %tok.1, bf16[7168,256]{1,0:T(8,128)(2,1)} %bitcast.5, bf16[7168,256]{1,0:T(8,128)(2,1)} %bitcast.6, bf16[256,7168]{1,0:T(8,128)(2,1)} %bitcast.7), custom_call_target="tpu_custom_call" | custom-call | tf_op jit(solution)/shard_map/moe/pallas_call | solution.py:420
  147.9 1.6 %copy.8 = bf16[128,896]{1,0:T(8,128)(2,1)} copy(bf16[128,896]{1,0:T(8,128)(2,1)} %moe.1) | data formatting | bytes 458752

commit v2 on v0

v2 whole, which is shorter than its diff:
```python
import jax
import jax.numpy as jnp
from jax import lax
from jax.experimental import pallas as pl
from jax.experimental.pallas import tpu as pltpu
from jax.sharding import PartitionSpec as P

MESH = pl.DeviceIdType.MESH
F32, BF16 = jnp.float32, jnp.bfloat16
D, REGION, CW, HW = 7168, 1792, 256, 128
TOK, CAP, NE, TOPK = 128, 24, 32, 4
NX, NZ, NY = 4, 8, 4
NB = 8
BR = 2 * CAP
SENT = NB * BR
ROWS = NB * CAP
HALF = ROWS // 2
NJ = REGION // CW
NU = 2 * NJ
NPIECE = 7
LX, LF, LM = 1, 3, 5
LP = NJ + LM
LA, LS, LC, LO = LP + 2, LP + 4, LP + 6, LP + 7


def kernel(ids_ref, score_ref, tok, gate, up, down, out_ref, wgu, wd, tokv, GS, PK, XA, acc, H, S, WW, PX, RA, FX, GB, Q, ZF, ZO, O,
           l_sem, w_send, w_recv, a_send, a_recv, x_send, x_recv, rx_send, rx_recv, b_send, b_recv, o_send, o_recv):
    pp, ep = lax.axis_index("pp"), lax.axis_index("ep")
    x, c, z, y = lax.div(pp, 2), lax.rem(pp, 2), lax.div(ep, NY), lax.rem(ep, NY)
    sgn = 2 * c - 1

    def dev(dx=0, dz=0, dy=0):
        return (lax.rem(x + dx + NX, NX) * 2 + c, lax.rem(z + dz + NZ, NZ) * NY + lax.rem(y + dy, NY))

    def remote(src, dst, ss, rs, device):
        return pltpu.make_async_remote_copy(src_ref=src, dst_ref=dst, send_sem=ss, recv_sem=rs, device_id=device,
                                            device_id_type=MESH)

    sib = (x * 2 + 1 - c, ep)
    bar = pltpu.get_barrier_semaphore()

    def greet(device):
        pl.semaphore_signal(bar, inc=1, device_id=device, device_id_type=MESH)

    for dx in (1, 2, 3):
        greet(dev(dx=dx))
    greet(sib)
    for dy in range(NY):
        for dz in (1, 2, 3, 5, 6, 7):
            greet(dev(dz=dz, dy=dy))

    @pl.when(c == 0)
    def _():
        for dy in range(1, NY):
            greet(dev(dy=dy))

    @pl.when(c == 1)
    def _():
        for dy in range(NY):
            greet(dev(dz=4, dy=dy))

    own_rows = pl.ds(pl.multiple_of(c * 256, 256), 256)
    tok_copy = pltpu.make_async_copy(tok, tokv, l_sem.at[3])
    local = [
        pltpu.make_async_copy(gate, wgu.at[c], l_sem.at[0]),
        pltpu.make_async_copy(up, wgu.at[2 + c], l_sem.at[1]),
        pltpu.make_async_copy(down, wd.at[own_rows], l_sem.at[2]),
    ]
    for cp in [tok_copy] + local:
        cp.start()

    ids, score = ids_ref[...].astype(F32), score_ref[...]
    e_iota = lax.broadcasted_iota(jnp.int32, (NE, TOK), 0).astype(F32)
    hot = [(e_iota == ids[k:k + 1, :]).astype(F32) for k in range(TOPK)]
    count = hot[0] + hot[1] + hot[2] + hot[3]
    before = (lax.broadcasted_iota(jnp.int32, (TOK, TOK), 0) < lax.broadcasted_iota(jnp.int32, (TOK, TOK), 1)).astype(F32)
    earlier = jnp.dot(count.astype(BF16), before.astype(BF16), preferred_element_type=F32)
    target = ids * CAP + jnp.concatenate([jnp.sum(h * earlier, axis=0, keepdims=True) for h in hot], axis=0)
    weight = score / jnp.sum(score, axis=0, keepdims=True)

    p_iota = lax.broadcasted_iota(jnp.int32, (CAP, TOK), 0).astype(F32)
    empty = jnp.zeros((CAP, TOK), F32)

    def slot_matches(g, k):
        expert = lax.rem(z + sgn * ((g if k % 2 == 0 else 3 - g) + c) + NZ, NZ) * NY + k // 2
        key = p_iota + (expert * CAP).astype(F32)
        return [(target[i:i + 1, :] == key).astype(F32) for i in range(TOPK)]

    def halves(a):
        return jnp.concatenate([jnp.concatenate([a, empty], axis=1), jnp.concatenate([empty, a], axis=1)], axis=0)

    def pick_slots(g):
        for k in range(NB):
            eq = slot_matches(g, k)
            at = g * SENT + k * BR
            S[at:at + BR, :] = halves(eq[0] + eq[1] + eq[2] + eq[3]).astype(BF16)

    def weigh_slots(g):
        rows = []
        for k in range(NB):
            eq = slot_matches(g, k)
            rows.append(halves(sum(eq[i] * weight[i:i + 1, :] for i in range(TOPK))))
        WW[:, g * SENT:(g + 1) * SENT] = jnp.concatenate(rows, axis=0).T.astype(BF16)

    pick_slots(0)

    def parts(u):
        return lax.div(u, NJ), lax.rem(u, NJ)

    def col(r, j):
        return pl.multiple_of(REGION * r + CW * j, CW)

    def block(k):
        return pl.ds(pl.multiple_of(k * BR, 16), BR)

    def scatter(src, dst, ss, rs, u, way):
        g = lax.div(u, NJ)
        whole = jnp.logical_or(c == 1, g == 1)
        for s2 in (1, 0):
            dz = way * sgn * ((3 - g if s2 else g) + c)
            for dy in range(NY):
                cp = remote(src.at[u, block(lax.rem(y + dy, NY) * 2 + s2)], dst.at[u, block(y * 2 + s2)], ss.at[u], rs.at[u],
                            dev(dz=dz, dy=dy))
                if s2 or dy:
                    cp.start()
                else:
                    pl.when(whole)(cp.start)

        @pl.when(jnp.logical_not(whole))
        def _():
            pltpu.make_async_copy(src.at[u, block(y * 2)], dst.at[u, block(y * 2)], rs.at[u]).start()

    def all_arrived(dst, rs, u):
        remote(dst.at[u], dst.at[u], rs.at[u], rs.at[u], sib).wait_recv()

    def all_left(src, ss, u):
        whole = jnp.logical_or(c == 1, lax.div(u, NJ) == 1)

        @pl.when(whole)
        def _():
            remote(src.at[u], src.at[u], ss.at[u], ss.at[u], sib).wait_send()

        @pl.when(jnp.logical_not(whole))
        def _():
            most = src.at[u, pl.ds(0, SENT - BR)]
            remote(most, most, ss.at[u], ss.at[u], sib).wait_send()

    def x_copy(i, u):
        if i < 2:
            return remote(XA.at[x, u], XA.at[x, u], x_send.at[i, u], x_recv.at[i, u], dev(dx=1 - 2 * i))
        away = lax.rem(x + (3 if i == 2 else 1), NX)
        part = pl.ds(0, HALF) if i == 2 else pl.ds(HALF, HALF)
        return remote(XA.at[away, u, part], XA.at[away, u, part], x_send.at[i, u], x_recv.at[i, u], dev(dx=1 if i == 2 else -1))

    right, left, anti = lax.rem(x + 1, NX), lax.rem(x + 3, NX), lax.rem(x + 2, NX)
    lo, hi = pl.ds(0, HALF), pl.ds(HALF, HALF)

    def rx_copy(i, u):
        src, dst, dx = [
            (PX.at[u, anti, lo], RA.at[0, u], 1),
            (PX.at[u, anti, hi], RA.at[1, u], -1),
            (PX.at[u, right, hi], FX.at[0, u, hi], 1),
            (PX.at[u, left, lo], FX.at[1, u, lo], -1),
            (PX.at[u, right, lo], FX.at[0, u, lo], 1),
            (PX.at[u, left, hi], FX.at[1, u, hi], -1),
        ][i]
        return remote(src, dst, rx_send.at[i, u], rx_recv.at[i, u], dev(dx=dx))

    def piece(h, j):
        return lax.div(2 * j + h, NPIECE), lax.rem(2 * j + h, NPIECE)

    def out_copy(h, j):
        place = piece(h, j)[1]
        return remote(ZO.at[j, pl.ds(h * TOK, TOK)], O.at[place], o_send.at[h, j], o_recv.at[place], sib)

    w_copies = [
        remote(gate, wgu.at[c], w_send.at[0], w_recv.at[0], sib),
        remote(up, wgu.at[2 + c], w_send.at[1], w_recv.at[1], sib),
        remote(down, wd.at[own_rows], w_send.at[2], w_recv.at[2], sib),
    ]

    def send_rows(u):
        g, j = parts(u)
        at = col(x, j)
        both = jnp.concatenate([tokv[:, pl.ds(at, HW)], tokv[:, pl.ds(pl.multiple_of(at + HW, HW), HW)]], axis=0)
        rows = pl.ds(pl.multiple_of(g * SENT, SENT), SENT)
        GS[u] = jnp.dot(S[rows, :], both, preferred_element_type=F32).astype(BF16)
        scatter(GS, PK, a_send, a_recv, u, 1)

    @pl.when(c == 0)
    def _():
        pl.semaphore_wait(bar, 4 + 27)

    @pl.when(c == 1)
    def _():
        pl.semaphore_wait(bar, 4 + 28)

    tok_copy.wait()
    send_rows(0)

    def step(t, carry):
        def unit(lag, f):
            u = t - lag

            @pl.when(jnp.logical_and(u >= 0, u < NU))
            def _():
                f(u)

        @pl.when(t < NU - 1)
        def _():
            send_rows(t + 1)

        @pl.when(t == 0)
        def _():
            for cp in w_copies:
                cp.start()
            acc[...] = jnp.zeros_like(acc)
            pick_slots(1)

        def forward(u):
            x_copy(0, u).wait()
            x_copy(2, u).start()
            x_copy(1, u).wait()
            x_copy(3, u).start()

        unit(LF, forward)

        def send_x(u):
            all_arrived(PK, a_recv, u)
            a = PK[u].astype(F32).reshape(NB, BR, HW)
            XA[x, u] = jnp.concatenate([a[:, :CAP].reshape(ROWS, HW), a[:, CAP:].reshape(ROWS, HW)], axis=1).astype(BF16)
            x_copy(0, u).start()
            x_copy(1, u).start()

        unit(LX, send_x)

        def add_x(u):
            rx_copy(0, u).wait()
            PX[u, right, lo, :] = (PX[u, right, lo, :].astype(F32) + RA[0, u].astype(F32)).astype(BF16)
            rx_copy(4, u).start()
            rx_copy(1, u).wait()
            PX[u, left, hi, :] = (PX[u, left, hi, :].astype(F32) + RA[1, u].astype(F32)).astype(BF16)
            rx_copy(5, u).start()

        unit(LA, add_x)

        @pl.when(jnp.logical_or(t == LP, t == LP + NJ))
        def _():
            g = lax.div(t - LP, NJ)
            for i in range(2):
                v = acc[g, i]
                H[g, :, i * 256:(i + 1) * 256] = (v / (1.0 + jnp.exp(-v)) * acc[g, 2 + i]).astype(BF16)

        @pl.when(t == LP)
        def _():
            local[2].wait()
            w_copies[2].wait()

        def down_part(u):
            g, j = parts(u)

            @pl.loop(0, NX)
            def _(i):
                r = lax.rem(x + 2 + i, NX)
                PX[u, r] = jnp.dot(H[g], wd[:, pl.ds(col(r, j), CW)], preferred_element_type=F32).astype(BF16)

            for i in range(4):
                rx_copy(i, u).start()

        unit(LP, down_part)

        def sum_x(u):
            for i in range(2, 6):
                rx_copy(i, u).wait()
            a = PX[u, x].astype(F32) + FX[0, u].astype(F32) + FX[1, u].astype(F32)
            a = jnp.concatenate([a[:, :HW].reshape(NB, CAP, HW), a[:, HW:].reshape(NB, CAP, HW)], axis=1)
            GB[u] = a.reshape(SENT, HW).astype(BF16)
            scatter(GB, Q, b_send, b_recv, u, -1)

        unit(LS, sum_x)

        @pl.when(t == 1)
        def _():
            weigh_slots(0)

        @pl.when(t == 2)
        def _():
            weigh_slots(1)

        @pl.when(t == LM)
        def _():
            for cp in local[:2] + w_copies[:2]:
                cp.wait()

        def gate_up(u):
            g, j = parts(u)
            x_copy(2, u).wait()
            x_copy(3, u).wait()

            @pl.loop(0, 4)
            def _(i):
                acc[g, i] += sum(jnp.dot(XA[r, u], wgu[i, pl.ds(col(r, j), CW), :], preferred_element_type=F32)
                                 for r in range(NX))

        unit(LM, gate_up)

        def combine(u):
            g, j = parts(u)
            all_arrived(Q, b_recv, u)
            cols = pl.ds(pl.multiple_of(g * SENT, SENT), SENT)
            part = jnp.dot(WW[:, cols], Q[u], preferred_element_type=F32)

            @pl.when(g == 0)
            def _():
                ZF[j] = part

            @pl.when(g == 1)
            def _():
                ZF[j] += part
                for h in range(2):
                    @pl.when(piece(h, j)[0] != c)
                    def _():
                        ZO[j, h * TOK:(h + 1) * TOK, :] = ZF[j, h * TOK:(h + 1) * TOK, :].astype(BF16)
                        out_copy(h, j).start()

        unit(LC, combine)

        def finish(u):
            j = u - NJ

            @pl.when(j >= 0)
            def _():
                for h in range(2):
                    core, place = piece(h, j)

                    @pl.when(core == c)
                    def _():
                        out_copy(h, j).wait_recv()
                        at = pl.ds(pl.multiple_of(place * HW, HW), HW)
                        out_ref[:, at] = (ZF[j, h * TOK:(h + 1) * TOK, :] + O[place].astype(F32)).astype(BF16)

                    @pl.when(core != c)
                    def _():
                        out_copy(h, j).wait_send()

        unit(LO, finish)
        unit(LX + 2, lambda u: all_left(GS, a_send, u))
        unit(LO, lambda u: all_left(GB, b_send, u))
        return carry

    lax.fori_loop(0, NU + LO, step, 0)


def per_device(tokens, expert_ids, route_score, gate_weight, up_weight, down_weight):
    vm, dma = pltpu.VMEM, pltpu.SemaphoreType.DMA
    hbm, here = pl.BlockSpec(memory_space=pl.ANY), pl.BlockSpec(memory_space=pltpu.VMEM)
    return pl.pallas_call(
        kernel,
        out_shape=jax.ShapeDtypeStruct((TOK, NPIECE * HW), BF16),
        in_specs=[here, here, hbm, hbm, hbm, hbm],
        out_specs=here,
        scratch_shapes=[
            vm((4, D, 256), BF16), vm((512, D), BF16), vm((TOK, D), BF16),
            vm((NU, SENT, HW), BF16), vm((NU, SENT, HW), BF16),
            vm((NX, NU, ROWS, CW), BF16),
            vm((2, 4, ROWS, 256), F32), vm((2, ROWS, 512), BF16),
            vm((2 * SENT, 2 * TOK), BF16), vm((2 * TOK, 2 * SENT), BF16),
            vm((NU, NX, ROWS, CW), BF16),
            vm((2, NU, HALF, CW), BF16), vm((2, NU, ROWS, CW), BF16),
            vm((NU, SENT, HW), BF16), vm((NU, SENT, HW), BF16),
            vm((NJ, 2 * TOK, HW), F32), vm((NJ, 2 * TOK, HW), BF16),
            vm((NPIECE, TOK, HW), BF16),
            dma((4,)), dma((3,)), dma((3,)), dma((NU,)), dma((NU,)), dma((4, NU)), dma((4, NU)),
            dma((6, NU)), dma((6, NU)), dma((NU,)), dma((NU,)), dma((2, NJ)), dma((NPIECE,)),
        ],
        compiler_params=pltpu.CompilerParams(collective_id=0, has_side_effects=True, vmem_limit_bytes=62 * 2**20),
        name="moe",
    )(expert_ids.T, route_score.T, tokens, gate_weight[0], up_weight[0], down_weight[0])


def solution(mesh):
    placed = (
        P("ep", None),
        P("ep", None),
        P("ep", None),
        P("ep", None, "pp"),
        P("ep", None, "pp"),
        P("ep", "pp", None),
    )
    return jax.shard_map(
        per_device, mesh=mesh, in_specs=placed, out_specs=P("ep", "pp"), check_vma=False
    )
```

time: 663 us -> 126 us (0.19)
  waiting for transfers between devices: 288 us -> 0 us
  blocking collectives: 253 us -> 0 us
  Pallas kernels: 0 us -> 125 us
  local copies, waits for them, and re-layouts: 57 us -> 1.65 us
  matrix products: 21.9 us -> 0 us
  other arithmetic: 21.4 us -> 0 us
  between operations: 13.5 us -> 0.01 us
    all_to_all x1 -> x0, blocking collectives: 253 us -> none  [per_device(): lax.all_to_all(outgoing.reshape(expert_count, capacity, model_width), 'ep...]
    all_to_all x1 -> x0, waiting for transfers between devices: 241 us -> none  [per_device(): lax.all_to_all(expert_part.reshape(expert_count, capacity, model_width),...]
    pallas_call x0 -> x1, Pallas kernels: none -> 125 us  [per_device(): pl.pallas_call(kernel, out_shape=jax.ShapeDtypeStruct((TOK, NPIECE * HW),...]
    unnamed x2 -> x0, waiting for transfers between devices: 47.3 us -> none
    gather x2 -> x0, local copies, waits for them, and re-layouts: 28.8 us -> none  [the longest x1 19.4 us: per_device(): returned.reshape(-1, model_width)[target].astype(jnp.float32)]
    dot_general x2 -> x0, matrix products: 21.9 us -> none  [the longest x1 18.9 us: per_device(): jnp.dot(hidden, down_local, preferred_element_type=jnp.float32)]
    convert_element_type x1 -> x0, local copies, waits for them, and re-layouts: 14.1 us -> none  [per_device(): picked = returned.reshape(-1, model_width)[target].astype(jnp.float32).re...]
    reduce_sum x3 -> x0, other arithmetic: 13.6 us -> none  [the longest x1 13.5 us: per_device(): blended = jnp.sum(picked * route_weight[:, :, None], axis=1)]
  transfers between devices with their start and end apart: 2 -> 0, of which waited for: 2 -> 0; matrix products, arithmetic and copies ran while one was open for 0% -> 0% of each run, Pallas kernels for 0% -> 0%
where the time goes in v2:
time: 126 us
  Pallas kernels  125 us (99%)
  local copies, waits for them, and re-layouts  1.65 us (1%)
    pallas_call x1, Pallas kernels, per_device(): pl.pallas_call(kernel, out_shape=jax.ShapeDtypeStruct((TOK, NPIECE * HW),...  125 us

profile of v2, /device:TPU:1, one launch (start us, length us, event | category | flops | bytes accessed | tf_op | source)
XLA Modules:
  0.0 126.2 jit_solution(9433035370288567844)
XLA Ops:
  0.0 124.6 %moe.1 = bf16[128,896]{1,0:T(8,128)(2,1)} custom-call(s32[4,128]{1,0:T(4,128)} %bitcast.8, f32[4,128]{1,0:T(4,128)} %bitcast.9, bf16[128,7168]{1,0:T(8,128)(2,1)} %tok.1, bf16[7168,256]{1,0:T(8,128)(2,1)} %bitcast.5, bf16[7168,256]{1,0:T(8,128)(2,1)} %bitcast.6, bf16[256,7168]{1,0:T(8,128)(2,1)} %bitcast.7), custom_call_target="tpu_custom_call" | custom-call | tf_op jit(solution)/shard_map/moe/pallas_call | solution.py:357
  124.6 1.6 %copy.8 = bf16[128,896]{1,0:T(8,128)(2,1)} copy(bf16[128,896]{1,0:T(8,128)(2,1)} %moe.1) | data formatting | bytes 458752

commit v3 on v2

--- a/solution.py
+++ b/solution.py
@@ -17,14 +17,23 @@
 HALF = ROWS // 2
 NJ = REGION // CW
 NU = 2 * NJ
+NK, NA = 6, 6
+NRA = NA - NK
+NR = NRA + NX * (NJ - NA)
+YR = 2 * CAP
+PLACE = (0, 2, 3, 1)
 NPIECE = 7
 LX, LF, LM = 1, 3, 5
 LP = NJ + LM
 LA, LS, LC, LO = LP + 2, LP + 4, LP + 6, LP + 7
+LD = 2
+RING = ((0, -1, 0), (1, -1, 2), (2, -1, 4), (3, -1, 6))
 
 
 def kernel(ids_ref, score_ref, tok, gate, up, down, out_ref, wgu, wd, tokv, GS, PK, XA, acc, H, S, WW, PX, RA, FX, GB, Q, ZF, ZO, O,
-           l_sem, w_send, w_recv, a_send, a_recv, x_send, x_recv, rx_send, rx_recv, b_send, b_recv, o_send, o_recv):
+           mine, metas, T, SR, GR,
+           l_sem, w_send, w_recv, a_send, a_recv, x_send, x_recv, rx_send, rx_recv, b_send, b_recv, o_send, o_recv,
+           m_send, m_recv, z_send, z_recv, y_send, y_recv):
     pp, ep = lax.axis_index("pp"), lax.axis_index("ep")
     x, c, z, y = lax.div(pp, 2), lax.rem(pp, 2), lax.div(ep, NY), lax.rem(ep, NY)
     sgn = 2 * c - 1
@@ -103,6 +112,8 @@
         WW[:, g * SENT:(g + 1) * SENT] = jnp.concatenate(rows, axis=0).T.astype(BF16)
 
     pick_slots(0)
+    mine[0:4, :] = target
+    mine[4:8, :] = weight
 
     def parts(u):
         return lax.div(u, NJ), lax.rem(u, NJ)
@@ -145,6 +156,64 @@
             most = src.at[u, pl.ds(0, SENT - BR)]
             remote(most, most, ss.at[u], ss.at[u], sib).wait_send()
 
+    def stage(s):
+        return pl.ds(PLACE[s] * TOK, TOK)
+
+    def hop(s, n, at):
+        src = tokv.at[:, pl.ds(at, CW)] if s == 0 else T.at[n, stage(s - 1)]
+        return remote(src, T.at[n, stage(s)], z_send.at[s, n], z_recv.at[s, n], dev(dz=sgn))
+
+    def start_hop(s, n, at):
+        if s == 0:
+            @pl.when(c == 0)
+            def _():
+                T[n, stage(0), :] = tokv[:, pl.ds(at, CW)]
+
+            @pl.when(c == 1)
+            def _():
+                hop(0, n, at).start()
+
+            return
+        if s == 1:
+            pl.when(c == 1)(lambda: hop(0, n, at).wait())
+        else:
+            hop(s - 1, n, at).wait()
+        hop(s, n, at).start()
+
+    def meta_copy(s):
+        return remote(mine, metas.at[s], m_send.at[s], m_recv.at[s], dev(dz=sgn * (s + c)))
+
+    def ring_slots():
+        @pl.when(c == 1)
+        def _():
+            meta_copy(0).wait()
+
+        for s in range(1, 4):
+            meta_copy(s).wait()
+        for g in range(2):
+            for s2 in range(2):
+                rows = []
+                for yy in range(NY):
+                    key = p_iota + ((z * NY + yy) * CAP).astype(F32)
+                    pick = sum((metas[3 - g if s2 else g, i:i + 1, :] == key).astype(F32) for i in range(TOPK))
+                    rows += [empty, pick] if s2 else [pick, empty]
+                SR[g, :, s2 * TOK:(s2 + 1) * TOK] = jnp.concatenate(rows, axis=0).astype(BF16)
+
+    def y_rows(k):
+        return pl.ds(pl.multiple_of(k * YR, 16), YR)
+
+    def y_copy(dy, g, n, u, r):
+        there = lax.rem(y + dy, NY)
+        return remote(GR.at[g, n, y_rows(there)], XA.at[r, u, y_rows(y)], y_send.at[dy - 1, g, n], y_recv.at[dy - 1, g, n],
+                      dev(dy=dy))
+
+    def ring_rows(g, n, u, r):
+        pair = pl.ds(pl.multiple_of(g * 2 * TOK, 2 * TOK), 2 * TOK)
+        GR[g, n] = jnp.dot(SR[g], T[n, pair, :], preferred_element_type=F32).astype(BF16)
+        for dy in range(1, NY):
+            y_copy(dy, g, n, u, r).start()
+        XA[r, u, y_rows(y), :] = GR[g, n, y_rows(y), :]
+
     def x_copy(i, u):
         if i < 2:
             return remote(XA.at[x, u], XA.at[x, u], x_send.at[i, u], x_recv.at[i, u], dev(dx=1 - 2 * i))
@@ -195,8 +264,23 @@
     def _():
         pl.semaphore_wait(bar, 4 + 28)
 
+    @pl.when(c == 0)
+    def _():
+        metas[0] = mine[...]
+
+    @pl.when(c == 1)
+    def _():
+        meta_copy(0).start()
+
+    for s in range(1, 4):
+        meta_copy(s).start()
     tok_copy.wait()
     send_rows(0)
+    send_rows(1)
+
+    @pl.loop(0, NRA)
+    def _(n):
+        start_hop(0, n, col(x, NK + n))
 
     def step(t, carry):
         def unit(lag, f):
@@ -206,9 +290,51 @@
             def _():
                 f(u)
 
-        @pl.when(t < NU - 1)
-        def _():
-            send_rows(t + 1)
+        @pl.when(jnp.logical_and(t < NU - 2, lax.rem(t + 2, NJ) < NK))
+        def _():
+            send_rows(t + 2)
+
+        for s, at_a, at_d in RING:
+            if s:
+                @pl.when(t == at_a)
+                def _():
+                    @pl.loop(0, NRA)
+                    def _(n):
+                        start_hop(s, n, col(x, NK + n))
+
+            @pl.when(t == at_d)
+            def _():
+                @pl.loop(NRA, NR)
+                def _(n):
+                    start_hop(s, n, col(lax.rem(n - NRA, NX), NA + lax.div(n - NRA, NX)))
+
+        @pl.when(t == NK - 1)
+        def _():
+            ring_slots()
+
+        def pick_gathered(u):
+            g, j = parts(u)
+
+            @pl.when(jnp.logical_and(j >= NK, j < NA))
+            def _():
+                n = j - NK
+                pl.when(g == 0)(lambda: hop(3, n, 0).wait())
+                ring_rows(g, n, u, x)
+
+        unit(0, pick_gathered)
+
+        def pick_direct(u):
+            g, j = parts(u)
+
+            @pl.when(j >= NA)
+            def _():
+                @pl.loop(0, NX)
+                def _(r):
+                    n = NRA + (j - NA) * NX + r
+                    pl.when(g == 0)(lambda: hop(3, n, 0).wait())
+                    ring_rows(g, n, u, r)
+
+        unit(LD, pick_direct)
 
         @pl.when(t == 0)
         def _():
@@ -223,16 +349,29 @@
             x_copy(1, u).wait()
             x_copy(3, u).start()
 
-        unit(LF, forward)
+        def gathered(f):
+            return lambda u: pl.when(lax.rem(u, NJ) < NA)(lambda: f(u))
+
 
         def send_x(u):
-            all_arrived(PK, a_recv, u)
-            a = PK[u].astype(F32).reshape(NB, BR, HW)
-            XA[x, u] = jnp.concatenate([a[:, :CAP].reshape(ROWS, HW), a[:, CAP:].reshape(ROWS, HW)], axis=1).astype(BF16)
+            g, j = parts(u)
+
+            @pl.when(j < NK)
+            def _():
+                all_arrived(PK, a_recv, u)
+                a = PK[u].astype(F32).reshape(NB, BR, HW)
+                XA[x, u] = jnp.concatenate([a[:, :CAP].reshape(ROWS, HW), a[:, CAP:].reshape(ROWS, HW)], axis=1).astype(BF16)
+
+            @pl.when(j >= NK)
+            def _():
+                for dy in range(1, NY):
+                    y_copy(dy, g, j - NK, u, x).wait()
+
             x_copy(0, u).start()
             x_copy(1, u).start()
 
-        unit(LX, send_x)
+        unit(LX, gathered(send_x))
+        unit(LF, gathered(forward))
 
         def add_x(u):
             rx_copy(0, u).wait()
@@ -294,8 +433,18 @@
 
         def gate_up(u):
             g, j = parts(u)
-            x_copy(2, u).wait()
-            x_copy(3, u).wait()
+
+            @pl.when(j < NA)
+            def _():
+                x_copy(2, u).wait()
+                x_copy(3, u).wait()
+
+            @pl.when(j >= NA)
+            def _():
+                @pl.loop(0, NX)
+                def _(r):
+                    for dy in range(1, NY):
+                        y_copy(dy, g, NRA + (j - NA) * NX + r, u, r).wait()
 
             @pl.loop(0, 4)
             def _(i):
@@ -344,7 +493,7 @@
                         out_copy(h, j).wait_send()
 
         unit(LO, finish)
-        unit(LX + 2, lambda u: all_left(GS, a_send, u))
+        unit(LX + 2, lambda u: pl.when(lax.rem(u, NJ) < NK)(lambda: all_left(GS, a_send, u)))
         unit(LO, lambda u: all_left(GB, b_send, u))
         return carry
 
@@ -370,8 +519,11 @@
             vm((NU, SENT, HW), BF16), vm((NU, SENT, HW), BF16),
             vm((NJ, 2 * TOK, HW), F32), vm((NJ, 2 * TOK, HW), BF16),
             vm((NPIECE, TOK, HW), BF16),
+            vm((8, TOK), F32), vm((4, 8, TOK), F32),
+            vm((NR, 4 * TOK, CW), BF16), vm((2, ROWS, 2 * TOK), BF16), vm((2, NR, ROWS, CW), BF16),
             dma((4,)), dma((3,)), dma((3,)), dma((NU,)), dma((NU,)), dma((4, NU)), dma((4, NU)),
             dma((6, NU)), dma((6, NU)), dma((NU,)), dma((NU,)), dma((2, NJ)), dma((NPIECE,)),
+            dma((4,)), dma((4,)), dma((4, NR)), dma((4, NR)), dma((3, 2, NR)), dma((3, 2, NR)),
         ],
         compiler_params=pltpu.CompilerParams(collective_id=0, has_side_effects=True, vmem_limit_bytes=62 * 2**20),
         name="moe",

time: 126 us -> 123 us (0.976)
  Pallas kernels: 125 us -> 121 us
    pallas_call x1, Pallas kernels: 125 us -> 121 us  [per_device(): pl.pallas_call(kernel, out_shape=jax.ShapeDtypeStruct((TOK, NPIECE * HW),...]
where the time goes in v3:
time: 123 us
  Pallas kernels  121 us (98%)
  local copies, waits for them, and re-layouts  1.65 us (1%)
    pallas_call x1, Pallas kernels, per_device(): pl.pallas_call(kernel, out_shape=jax.ShapeDtypeStruct((TOK, NPIECE * HW),...  121 us

profile of v3, /device:TPU:1, one launch (start us, length us, event | category | flops | bytes accessed | tf_op | source)
XLA Modules:
  0.0 122.7 jit_solution(18351816618869689346)
XLA Ops:
  0.0 121.0 %moe.1 = bf16[128,896]{1,0:T(8,128)(2,1)} custom-call(s32[4,128]{1,0:T(4,128)} %bitcast.8, f32[4,128]{1,0:T(4,128)} %bitcast.9, bf16[128,7168]{1,0:T(8,128)(2,1)} %tok.1, bf16[7168,256]{1,0:T(8,128)(2,1)} %bitcast.5, bf16[7168,256]{1,0:T(8,128)(2,1)} %bitcast.6, bf16[256,7168]{1,0:T(8,128)(2,1)} %bitcast.7), custom_call_target="tpu_custom_call" | custom-call | tf_op jit(solution)/shard_map/moe/pallas_call | solution.py:506
  121.0 1.6 %copy.8 = bf16[128,896]{1,0:T(8,128)(2,1)} copy(bf16[128,896]{1,0:T(8,128)(2,1)} %moe.1) | data formatting | bytes 458752

commit v4 on v3

--- a/solution.py
+++ b/solution.py
@@ -23,7 +23,7 @@
 YR = 2 * CAP
 PLACE = (0, 2, 3, 1)
 NPIECE = 7
-LX, LF, LM = 1, 3, 5
+LX, LF, LM = 1, 3, 6
 LP = NJ + LM
 LA, LS, LC, LO = LP + 2, LP + 4, LP + 6, LP + 7
 LD = 2
@@ -403,8 +403,13 @@
                 r = lax.rem(x + 2 + i, NX)
                 PX[u, r] = jnp.dot(H[g], wd[:, pl.ds(col(r, j), CW)], preferred_element_type=F32).astype(BF16)
 
-            for i in range(4):
-                rx_copy(i, u).start()
+                @pl.when(i == 0)
+                def _():
+                    rx_copy(0, u).start()
+                    rx_copy(1, u).start()
+
+                pl.when(i == 1)(lambda: rx_copy(3, u).start())
+                pl.when(i == 3)(lambda: rx_copy(2, u).start())
 
         unit(LP, down_part)
 

time: 123 us -> 123 us (level)
  no operation moved by 1% of the time
where the time goes in v4:
time: 123 us
  Pallas kernels  121 us (98%)
  local copies, waits for them, and re-layouts  1.65 us (1%)
    pallas_call x1, Pallas kernels, per_device(): pl.pallas_call(kernel, out_shape=jax.ShapeDtypeStruct((TOK, NPIECE * HW),...  121 us

profile of v4, /device:TPU:1, one launch (start us, length us, event | category | flops | bytes accessed | tf_op | source)
XLA Modules:
  0.0 122.6 jit_solution(7755159621355677943)
XLA Ops:
  0.0 120.9 %moe.1 = bf16[128,896]{1,0:T(8,128)(2,1)} custom-call(s32[4,128]{1,0:T(4,128)} %bitcast.8, f32[4,128]{1,0:T(4,128)} %bitcast.9, bf16[128,7168]{1,0:T(8,128)(2,1)} %tok.1, bf16[7168,256]{1,0:T(8,128)(2,1)} %bitcast.5, bf16[7168,256]{1,0:T(8,128)(2,1)} %bitcast.6, bf16[256,7168]{1,0:T(8,128)(2,1)} %bitcast.7), custom_call_target="tpu_custom_call" | custom-call | tf_op jit(solution)/shard_map/moe/pallas_call | solution.py:511
  120.9 1.6 %copy.8 = bf16[128,896]{1,0:T(8,128)(2,1)} copy(bf16[128,896]{1,0:T(8,128)(2,1)} %moe.1) | data formatting | bytes 458752
